TPU v7x, 128 devices: a whole 4x4x4 slice. The times are simulated.
128 devices in a mesh: row: 16 (over x, z), col: 8 (over y, core).
Axes of the slice: x: 4, y: 4, z: 4, core: 2. Of those that a mesh axis runs over, the one named last changes fastest.
Arguments:
- snapshots: bfloat16 [512, 524288], P(('row', 'col')), may hold values from -60 to 60, as said below
- block_order: int32 [1024], replicated, may hold values from 0 to 1023, each once
Outputs:
- scaled_factor: float32 [512, 512], replicated
- basis: float32 [512, 524288], P(None, ('row', 'col'))
Inputs may be any that keep to these rules, and one draw needn't show every extreme that they name: `block_order`: every block index appears exactly once. `snapshots`: entries stay within the range.
All inputs are finite; a program needn't handle non-finite values.
Results may differ from a plain program's by a relative error of at most 0.0003.
The roundings to bfloat16 on the way count: a program that leaves them out, or rounds other values in their place, can miss the bound.
Values may be sent and summed in bfloat16 or wider, within the bound.
A program may use at most 128 MiB of HBM per device.

v0:
```python
import math, functools
import jax, jax.numpy as jnp
from jax import lax
from jax.experimental import pallas as pl
from jax.experimental.pallas import tpu as pltpu
from jax.sharding import PartitionSpec as P

TILE = 128
GROUP = 4
CHUNK = 512
EXACT = lax.Precision.HIGHEST


def factor_tile(work):
    lanes = lax.broadcasted_iota(jnp.int32, (8, TILE), 1)
    subs = lax.broadcasted_iota(jnp.int32, (8, TILE), 0)
    nslab = TILE // 8
    left = [work[8 * s : 8 * s + 8, :] for s in range(nslab)]
    right = [(lanes == subs + 8 * s).astype(jnp.float32) for s in range(nslab)]
    upper_rows, inverse_rows = [], []
    for start in range(0, TILE, GROUP):
        slab, base = start // 8, start % 8
        rows = [jnp.broadcast_to(left[slab][base + k : base + k + 1, :], (8, TILE)) for k in range(GROUP)]
        sides = [jnp.broadcast_to(right[slab][base + k : base + k + 1, :], (8, TILE)) for k in range(GROUP)]
        columns = [
            [jnp.broadcast_to(left[s][:, start + k : start + k + 1], (8, TILE)) for k in range(GROUP)]
            for s in range(slab, nslab)
        ]
        corner = [
            [jnp.broadcast_to(rows[k][:, start + l : start + l + 1], (8, TILE)) if l >= k else None for l in range(GROUP)]
            for k in range(GROUP)
        ]
        scales, inverses, scaled_rows, scaled_sides = [], [], [], []
        for k in range(GROUP):
            pivot = corner[k][k]
            guess = lax.rsqrt(pivot)
            root = guess * (1.5 - (0.5 * pivot) * guess * guess)
            reciprocal = root * root
            ratios = [corner[k][l] * reciprocal for l in range(k + 1, GROUP)]
            for l in range(k + 1, GROUP):
                ratio = ratios[l - k - 1]
                for m in range(l, GROUP):
                    corner[l][m] = corner[l][m] - ratio * corner[k][m]
                rows[l] = rows[l] - ratio * rows[k]
                sides[l] = sides[l] - ratio * sides[k]
                for column in columns:
                    column[l] = column[l] - ratio * column[k]
            upper_rows.append(rows[k][:1, :] * root[:1, :])
            inverse_rows.append(sides[k][:1, :] * root[:1, :])
            scaled_rows.append(rows[k] * reciprocal)
            scaled_sides.append(sides[k] * reciprocal)
        first = slab + (1 if base + GROUP == 8 else 0)
        for s in range(first, nslab):
            column = columns[s - slab]
            new_left, new_right = left[s], right[s]
            for k in range(GROUP):
                new_left = new_left - column[k] * scaled_rows[k]
                new_right = new_right - column[k] * scaled_sides[k]
            left[s], right[s] = new_left, new_right
    upper = jnp.concatenate(upper_rows, axis=0)
    inverse = jnp.concatenate(inverse_rows, axis=0)
    return upper, inverse


def mul(a, b):
    return lax.dot_general(a, b, (((1,), (0,)), ((), ())), precision=EXACT, preferred_element_type=jnp.float32)


def mul_t(a, b):
    return lax.dot_general(a, b, (((0,), (0,)), ((), ())), precision=EXACT, preferred_element_type=jnp.float32)


def factor_kernel(gram, owned_hbm, factor, basis_hbm, work, side, owned, basis, owned_sem, basis_sem, *, root):
    size, width = owned.shape
    fetch = pltpu.make_async_copy(owned_hbm, owned, owned_sem)
    fetch.start()
    work[...] = gram[...]
    panels = size // TILE
    stores = []
    for p in range(panels):
        lo, hi = p * TILE, (p + 1) * TILE
        upper, inverse = factor_tile(work[lo:hi, lo:hi])
        rows = lax.broadcasted_iota(jnp.int32, (TILE, TILE), 0)
        lanes = lax.broadcasted_iota(jnp.int32, (TILE, TILE), 1)
        factor[lo:hi, lo:hi] = jnp.where(lanes >= rows, upper, 0.0) / root
        if p:
            factor[lo:hi, :lo] = jnp.zeros((TILE, lo), jnp.float32)
            inverse = jnp.concatenate([mul(inverse, side[lo:hi, :lo]), inverse], axis=1)
        if hi < size:
            cross = mul(inverse[:, lo:hi], work[lo:hi, hi:])
            factor[lo:hi, hi:] = cross / root
            work[hi:, hi:] = work[hi:, hi:] - mul_t(cross, cross)
            update = -mul_t(cross, inverse)
            if p:
                side[hi:, :lo] = side[hi:, :lo] + update[:, :lo]
            side[hi:, lo:hi] = update[:, lo:hi]
        if p == 0:
            fetch.wait()
        narrow = (inverse * root).astype(jnp.bfloat16)

        def columns(c, carry, narrow=narrow, lo=lo, hi=hi):
            at = pl.ds(pl.multiple_of(c * CHUNK, CHUNK), CHUNK)
            basis[lo:hi, at] = jnp.dot(narrow, owned[:hi, at], preferred_element_type=jnp.float32)
            return carry

        lax.fori_loop(0, width // CHUNK, columns, 0)
        store = pltpu.make_async_copy(basis.at[lo:hi, :], basis_hbm.at[lo:hi, :], basis_sem.at[p])
        store.start()
        stores.append(store)
    for store in stores:
        store.wait()


def factor_and_basis(gram, owned, total_rows):
    size, width = owned.shape
    return pl.pallas_call(
        functools.partial(factor_kernel, root=math.sqrt(total_rows)),
        out_shape=(
            jax.ShapeDtypeStruct((size, size), jnp.float32),
            jax.ShapeDtypeStruct((size, width), jnp.float32),
        ),
        in_specs=[pl.BlockSpec(memory_space=pltpu.VMEM), pl.BlockSpec(memory_space=pl.ANY)],
        out_specs=(pl.BlockSpec(memory_space=pltpu.VMEM), pl.BlockSpec(memory_space=pl.ANY)),
        scratch_shapes=[
            pltpu.VMEM((size, size), jnp.float32),
            pltpu.VMEM((size, size), jnp.float32),
            pltpu.VMEM((size, width), jnp.bfloat16),
            pltpu.VMEM((size, width), jnp.float32),
            pltpu.SemaphoreType.DMA,
            pltpu.SemaphoreType.DMA((size // TILE,)),
        ],
        compiler_params=pltpu.CompilerParams(vmem_limit_bytes=40 * 2**20),
        name="factor_and_basis",
    )(gram, owned)


def sum_over_devices(local, devices):
    size = local.shape[0]
    share = local.reshape(devices, -1, 128)
    parts = lax.all_to_all(share, ("row", "col"), split_axis=0, concat_axis=0, tiled=True)
    total = jnp.sum(parts, axis=0)
    spread = jnp.broadcast_to(total[None], parts.shape)
    whole = lax.all_to_all(spread, ("row", "col"), split_axis=0, concat_axis=0, tiled=True)
    return whole.reshape(size, size)


def per_device(snapshots, block_order, devices):
    local_count = snapshots.shape[0]
    total_rows = snapshots.shape[1]
    nblocks = block_order.shape[0]
    block_rows = total_rows // nblocks
    reordered = snapshots.reshape(local_count, nblocks, block_rows)[:, block_order, :].reshape(
        local_count, total_rows
    )
    owned = lax.all_to_all(reordered, ("row", "col"), split_axis=1, concat_axis=0, tiled=True)
    gram = jnp.dot(owned, owned.T, preferred_element_type=jnp.float32)
    summed = sum_over_devices(gram, devices)
    return factor_and_basis(summed, owned, total_rows)


def solution(mesh):
    placed = (P(("row", "col"), None), P())
    return jax.shard_map(
        functools.partial(per_device, devices=mesh.size),
        mesh=mesh,
        in_specs=placed,
        out_specs=(P(), P(None, ("row", "col"))),
        check_vma=False,
    )
```

profile of v0, /device:TPU:1, one launch (start us, length us, event | category | flops | bytes accessed | tf_op | source)
XLA Modules:
  0.0 182.3 jit_solution(2576950257097219445)
XLA Ops:
  0.6 0.7 fusion
  1.3 12.9 %gather_fusion = bf16[1024,4,512]{2,1,0:T(4,128)(2,1)} fusion(bf16[4,1024,512]{2,0,1:T(4,128)(2,1)} %bitcast.9, s32[1024]{0:T(1024)S(1)} %fusion), kind=kCustom, calls=%fused_computation | custom fusion | bytes 8392704 | tf_op jit(solution)/shard_map/gather | solution.py:152
  14.2 64.5 %all_to_all.29 = bf16[4,128,4096]{2,0,1:T(4,128)(2,1)} all-to-all(bf16[4,128,4096]{2,0,1:T(4,128)(2,1)} %bitcast.8), channel_id=1, replica_groups=mesh['row'=16,'col'=8] {'row','col'}, dimensions={1} | all-to-all | bytes 8388608 | tf_op jit(solution)/shard_map/all_to_all | solution.py:155
  78.7 6.9 %all_to_all.23.owned_hbm = bf16[512,4096]{1,0:T(8,128)(2,1)} reshape(bf16[128,4,4096]{2,1,0:T(4,128)(2,1)} %bitcast.7) | data formatting | bytes 8388608 | tf_op jit(solution)/shard_map/all_to_all | solution.py:155
  85.6 5.8 %fusion.1 = f32[512,512]{1,0:T(8,128)S(1)} fusion(bf16[512,4096]{1,0:T(8,128)(2,1)} %all_to_all.23.owned_hbm), kind=kOutput, calls=%fused_computation.3 | convolution fusion | flops 2147483648 | bytes 5242880 | tf_op jit(solution)/shard_map/dot_general | solution.py:156
  91.4 0.1 reshape.20
  91.5 24.5 %all_to_all.30 = f32[128,16,128]{2,1,0:T(8,128)S(1)} all-to-all(f32[128,16,128]{2,1,0:T(8,128)S(1)} %reshape.20), channel_id=1, replica_groups=mesh['row'=16,'col'=8] {'row','col'}, dimensions={0} | all-to-all | bytes 2097152 | tf_op jit(solution)/shard_map/all_to_all | solution.py:140
  116.0 0.1 reduce_sum.9
  116.1 0.1 broadcast_in_dim.10
  116.2 23.6 %all_to_all.31 = f32[128,16,128]{2,1,0:T(8,128)S(1)} all-to-all(f32[128,16,128]{2,1,0:T(8,128)S(1)} %broadcast_in_dim.10), channel_id=1, replica_groups=mesh['row'=16,'col'=8] {'row','col'}, dimensions={0} | all-to-all | bytes 2097152 | tf_op jit(solution)/shard_map/all_to_all | solution.py:143
  139.8 0.2 reshape.21.gram
  139.9 0.0 copy-start
  139.9 2.2 %copy-done = bf16[512,4096]{1,0:T(8,128)(2,1)S(1)} copy-done((bf16[512,4096]{1,0:T(8,128)(2,1)S(1)}, bf16[512,4096]{1,0:T(8,128)(2,1)}, u32[]{:S(2)}) %copy-start) | copy-done | bytes 4194328
  142.1 40.0 %factor_and_basis.1 = (f32[512,512]{1,0:T(8,128)}, f32[512,4096]{1,0:T(8,128)}) custom-call(f32[512,512]{1,0:T(8,128)S(1)} %reshape.21.gram, bf16[512,4096]{1,0:T(8,128)(2,1)S(1)} %copy-done), custom_call_target="tpu_custom_call" | custom-call | tf_op jit(solution)/shard_map/factor_and_basis/pallas_call | solution.py:116
Async XLA Ops:
  139.9 2.2 %copy-start = (bf16[512,4096]{1,0:T(8,128)(2,1)S(1)}, bf16[512,4096]{1,0:T(8,128)(2,1)}, u32[]{:S(2)}) copy-start(bf16[512,4096]{1,0:T(8,128)(2,1)} %all_to_all.23.owned_hbm) | copy-start | bytes 12582916
where the time goes:
time: 183 us; the launch traced here: 182 us
  blocking collectives  113 us (62%)
  Pallas kernels  40 us (22%)
  local copies, waits for them, and re-layouts  22.3 us (12%)
  matrix products  5.82 us (3%)
    all_to_all x1, blocking collectives, per_device(): lax.all_to_all(reordered, ('row', 'col'), split_axis=1, concat_axis=0, ti...  64.5 us
    pallas_call x1, Pallas kernels, factor_and_basis(): pl.pallas_call(functools.partial(factor_kernel, root=math.sqrt(total_rows...  40 us
    all_to_all x1, blocking collectives, sum_over_devices(): lax.all_to_all(share, ('row', 'col'), split_axis=0, concat_axis=0, tiled=...  24.5 us
    all_to_all x1, blocking collectives, sum_over_devices(): lax.all_to_all(spread, ('row', 'col'), split_axis=0, concat_axis=0, tiled...  23.6 us
    gather x1, local copies, waits for them, and re-layouts, per_device(): snapshots.reshape(local_count, nblocks, block_rows)[:, block_order, :]  12.9 us
    all_to_all x1, local copies, waits for them, and re-layouts, per_device(): lax.all_to_all(reordered, ('row', 'col'), split_axis=1, concat_axis=0, ti...  6.87 us
    dot_general x1, matrix products, per_device(): gram = jnp.dot(owned, owned.T, preferred_element_type=jnp.float32)  5.82 us

commit v1 on v0

--- a/solution.py
+++ b/solution.py
@@ -8,6 +8,8 @@
 TILE = 128
 GROUP = 4
 CHUNK = 512
+VMEM_BYTES = 56 * 2**20
+MESH = pl.DeviceIdType.MESH
 EXACT = lax.Precision.HIGHEST
 
 
@@ -129,31 +131,248 @@
             pltpu.SemaphoreType.DMA,
             pltpu.SemaphoreType.DMA((size // TILE,)),
         ],
-        compiler_params=pltpu.CompilerParams(vmem_limit_bytes=40 * 2**20),
+        compiler_params=pltpu.CompilerParams(vmem_limit_bytes=VMEM_BYTES),
         name="factor_and_basis",
     )(gram, owned)
 
 
-def sum_over_devices(local, devices):
-    size = local.shape[0]
-    share = local.reshape(devices, -1, 128)
-    parts = lax.all_to_all(share, ("row", "col"), split_axis=0, concat_axis=0, tiled=True)
-    total = jnp.sum(parts, axis=0)
-    spread = jnp.broadcast_to(total[None], parts.shape)
-    whole = lax.all_to_all(spread, ("row", "col"), split_axis=0, concat_axis=0, tiled=True)
-    return whole.reshape(size, size)
+def position():
+    row, col = lax.axis_index("row"), lax.axis_index("col")
+    x, y = lax.div(row, 4), lax.div(col, 2)
+    return row, col, x, row - 4 * x, y, col - 2 * y
+
+
+def wrap(place):
+    return jnp.where(place >= 4, place - 4, place)
+
+
+def each_partner(place, both, visit):
+    row, col, x, z, y, core = place
+    ring = [y] + [wrap(y + d) for d in range(1, 4)]
+    cores = [core, 1 - core] if both else [core]
+
+    def turn(step, carry):
+        outer = lax.div(step, 4)
+        from_x, from_z = wrap(x + outer), wrap(z + step - 4 * outer)
+        for d in range(4):
+            there_row = wrap(from_x + d) * 4 + wrap(from_z + (4 - d) % 4)
+            for c, there_core in enumerate(cores):
+                there = (there_row, ring[d] * 2 + there_core)
+                if d or c:
+                    visit(there)
+                else:
+                    pl.when(step > 0)(functools.partial(visit, there))
+        return carry
+
+    lax.fori_loop(0, 16, turn, 0)
+
+
+def exchange_kernel(order, snapshots_hbm, arrived, snapshots, staged, fetch_sem, own_sem, send_sem, recv_sem):
+    place = position()
+    count, _, width = staged.shape
+    mine = place[0] * 8 + place[1]
+    block = snapshots.shape[2]
+    each = width // block
+    fetch = pltpu.make_async_copy(snapshots_hbm, snapshots, fetch_sem)
+    fetch.start()
+    barrier = pltpu.get_barrier_semaphore()
+
+    def greet(there):
+        pl.semaphore_signal(barrier, inc=1, device_id=there, device_id_type=MESH)
+
+    each_partner(place, True, greet)
+    fetch.wait()
+
+    def gather(there, carry):
+        for k in range(each):
+            staged[there, :, k * block : (k + 1) * block] = snapshots[order[there * each + k]]
+        return carry
+
+    lax.fori_loop(0, count, gather, 0)
+    pl.semaphore_wait(barrier, count - 1)
+
+    def send(there):
+        pltpu.make_async_remote_copy(
+            src_ref=staged.at[there[0] * 8 + there[1]],
+            dst_ref=arrived.at[mine],
+            send_sem=send_sem,
+            recv_sem=recv_sem,
+            device_id=there,
+            device_id_type=MESH,
+        ).start()
+
+    each_partner(place, True, send)
+    own = pltpu.make_async_copy(staged.at[mine], arrived.at[mine], own_sem)
+    own.start()
+    own.wait()
+    others = staged.at[pl.ds(0, count - 1)]
+    pltpu.make_async_copy(others, others, send_sem).wait()
+    pltpu.make_async_copy(others, others, recv_sem).wait()
+
+
+def exchange(snapshots, block_order, devices):
+    nblocks, local_count, block_rows = snapshots.shape
+    shape = (devices, local_count, nblocks * block_rows // devices)
+    return pl.pallas_call(
+        exchange_kernel,
+        out_shape=jax.ShapeDtypeStruct(shape, snapshots.dtype),
+        in_specs=[pl.BlockSpec(memory_space=pltpu.SMEM), pl.BlockSpec(memory_space=pl.ANY)],
+        out_specs=pl.BlockSpec(memory_space=pl.ANY),
+        scratch_shapes=[
+            pltpu.VMEM(snapshots.shape, snapshots.dtype),
+            pltpu.VMEM(shape, snapshots.dtype),
+            pltpu.SemaphoreType.DMA,
+            pltpu.SemaphoreType.DMA,
+            pltpu.SemaphoreType.DMA,
+            pltpu.SemaphoreType.DMA,
+        ],
+        compiler_params=pltpu.CompilerParams(
+            collective_id=0, has_side_effects=True, vmem_limit_bytes=VMEM_BYTES
+        ),
+        name="exchange",
+    )(block_order, snapshots)
+
+
+def gram_kernel(arrived, owned, gram):
+    step = pl.program_id(0)
+    count, depth, width = arrived.shape
+    block = arrived[...].reshape(count * depth, width)
+    owned[...] = block
+    part = lax.dot_general(block, block, (((1,), (1,)), ((), ())), preferred_element_type=jnp.float32)
+
+    @pl.when(step == 0)
+    def _():
+        gram[...] = part
+
+    @pl.when(step > 0)
+    def _():
+        gram[...] = gram[...] + part
+
+
+def local_gram(arrived):
+    count, depth, width = arrived.shape
+    size = count * depth
+    return pl.pallas_call(
+        gram_kernel,
+        grid=(width // CHUNK,),
+        out_shape=(
+            jax.ShapeDtypeStruct((size, width), arrived.dtype),
+            jax.ShapeDtypeStruct((size, size), jnp.float32),
+        ),
+        in_specs=[pl.BlockSpec((count, depth, CHUNK), lambda s: (0, 0, s))],
+        out_specs=(pl.BlockSpec((size, CHUNK), lambda s: (0, s)), pl.BlockSpec((size, size), lambda s: (0, 0))),
+        compiler_params=pltpu.CompilerParams(vmem_limit_bytes=VMEM_BYTES),
+        name="local_gram",
+    )(arrived)
+
+
+def sum_kernel(gram, total, half, parts, part, pair_send, pair_recv, send_sem, recv_sem, back_send, back_recv, last_send, last_recv):
+    place = position()
+    row, col, x, z, y, core = place
+    size = gram.shape[0]
+    middle = size // 2
+    chips = parts.shape[0]
+    sibling = (row, 2 * y + 1 - core)
+    chip = row * 4 + y
+
+    barrier = pltpu.get_barrier_semaphore()
+
+    def greet(there):
+        pl.semaphore_signal(barrier, inc=1, device_id=there, device_id_type=MESH)
+
+    greet(sibling)
+    each_partner(place, False, greet)
+    pl.semaphore_wait(barrier, chips)
+
+    mine = pl.multiple_of(core * middle, middle)
+    theirs = pl.multiple_of((1 - core) * middle, middle)
+    pair = pltpu.make_async_remote_copy(
+        src_ref=gram.at[pl.ds(theirs, middle)],
+        dst_ref=half,
+        send_sem=pair_send,
+        recv_sem=pair_recv,
+        device_id=sibling,
+        device_id_type=MESH,
+    )
+    pair.start()
+    pair.wait()
+    half[...] = half[...] + gram[pl.ds(mine, middle), :]
+
+    def send(there):
+        top, left = pl.multiple_of(there[0] * 16, 16), pl.multiple_of((there[1] - core) * 64, 128)
+        pltpu.make_async_remote_copy(
+            src_ref=half.at[pl.ds(top, 16), pl.ds(left, 128)],
+            dst_ref=parts.at[chip],
+            send_sem=send_sem,
+            recv_sem=recv_sem,
+            device_id=there,
+            device_id_type=MESH,
+        ).start()
+
+    each_partner(place, False, send)
+    top, left = pl.multiple_of(row * 16, 16), pl.multiple_of(y * 128, 128)
+    parts[chip] = half[pl.ds(top, 16), pl.ds(left, 128)]
+    others = parts.at[pl.ds(0, chips - 1)]
+    pltpu.make_async_copy(others, others, send_sem).wait()
+    pltpu.make_async_copy(others, others, recv_sem).wait()
+    sum_parts = parts[0]
+    for k in range(1, chips):
+        sum_parts = sum_parts + parts[k]
+    part[...] = sum_parts
+    total[pl.ds(mine + top, 16), pl.ds(left, 128)] = sum_parts
+
+    def back(there):
+        pltpu.make_async_remote_copy(
+            src_ref=part,
+            dst_ref=total.at[pl.ds(mine + top, 16), pl.ds(left, 128)],
+            send_sem=back_send,
+            recv_sem=back_recv,
+            device_id=there,
+            device_id_type=MESH,
+        ).start()
+
+    each_partner(place, False, back)
+    pltpu.make_async_copy(others, others, back_send).wait()
+    pltpu.make_async_copy(others, others, back_recv).wait()
+    last = pltpu.make_async_remote_copy(
+        src_ref=total.at[pl.ds(mine, middle)],
+        dst_ref=total.at[pl.ds(mine, middle)],
+        send_sem=last_send,
+        recv_sem=last_recv,
+        device_id=sibling,
+        device_id_type=MESH,
+    )
+    last.start()
+    last.wait()
+
+
+def sum_over_devices(gram, devices):
+    size = gram.shape[0]
+    chips = devices // 2
+    return pl.pallas_call(
+        sum_kernel,
+        out_shape=jax.ShapeDtypeStruct(gram.shape, gram.dtype),
+        in_specs=[pl.BlockSpec(memory_space=pltpu.VMEM)],
+        out_specs=pl.BlockSpec(memory_space=pltpu.VMEM),
+        scratch_shapes=[
+            pltpu.VMEM((size // 2, size), gram.dtype),
+            pltpu.VMEM((chips, 16, 128), gram.dtype),
+            pltpu.VMEM((16, 128), gram.dtype),
+        ]
+        + [pltpu.SemaphoreType.DMA] * 8,
+        compiler_params=pltpu.CompilerParams(
+            collective_id=1, has_side_effects=True, vmem_limit_bytes=VMEM_BYTES
+        ),
+        name="sum_over_devices",
+    )(gram)
 
 
 def per_device(snapshots, block_order, devices):
-    local_count = snapshots.shape[0]
-    total_rows = snapshots.shape[1]
+    local_count, total_rows = snapshots.shape
     nblocks = block_order.shape[0]
-    block_rows = total_rows // nblocks
-    reordered = snapshots.reshape(local_count, nblocks, block_rows)[:, block_order, :].reshape(
-        local_count, total_rows
-    )
-    owned = lax.all_to_all(reordered, ("row", "col"), split_axis=1, concat_axis=0, tiled=True)
-    gram = jnp.dot(owned, owned.T, preferred_element_type=jnp.float32)
+    blocks = snapshots.reshape(local_count, nblocks, total_rows // nblocks).transpose(1, 0, 2)
+    arrived = exchange(blocks, block_order, devices)
+    owned, gram = local_gram(arrived)
     summed = sum_over_devices(gram, devices)
     return factor_and_basis(summed, owned, total_rows)
 

time: 183 us -> 145 us (0.79)
  blocking collectives: 113 us -> 0 us
  Pallas kernels: 40 us -> 144 us
  local copies, waits for them, and re-layouts: 22.3 us -> 0 us
  matrix products: 5.82 us -> 0 us
    all_to_all x3 -> x0, blocking collectives: 113 us -> none  [the longest x1 64.5 us: per_device(): lax.all_to_all(reordered, ('row', 'col'), split_axis=1, concat_axis=0, ti...]
    pallas_call x0 -> x3, Pallas kernels: none -> 102 us  [the longest x1 61.2 us: exchange(): pl.pallas_call(exchange_kernel, out_shape=jax.ShapeDtypeStruct(shape, sna...]
    gather x1 -> x0, local copies, waits for them, and re-layouts: 12.9 us -> none  [per_device(): snapshots.reshape(local_count, nblocks, block_rows)[:, block_order, :]]
    all_to_all x1 -> x0, local copies, waits for them, and re-layouts: 6.87 us -> none  [per_device(): lax.all_to_all(reordered, ('row', 'col'), split_axis=1, concat_axis=0, ti...]
    dot_general x1 -> x0, matrix products: 5.82 us -> none  [per_device(): gram = jnp.dot(owned, owned.T, preferred_element_type=jnp.float32)]
    unnamed x2 -> x0, local copies, waits for them, and re-layouts: 2.18 us -> none
    pallas_call x1, Pallas kernels: 40 us -> 41.9 us  [factor_and_basis(): pl.pallas_call(functools.partial(factor_kernel, root=math.sqrt(total_rows...]
where the time goes in v1:
time: 145 us; the launch traced here: 144 us
  Pallas kernels  144 us (99%)
    pallas_call x1, Pallas kernels, exchange(): pl.pallas_call(exchange_kernel, out_shape=jax.ShapeDtypeStruct(shape, sna...  61.2 us
    pallas_call x1, Pallas kernels, factor_and_basis(): pl.pallas_call(functools.partial(factor_kernel, root=math.sqrt(total_rows...  41.9 us
    pallas_call x1, Pallas kernels, sum_over_devices(): pl.pallas_call(sum_kernel, out_shape=jax.ShapeDtypeStruct(gram.shape, gra...  31.5 us
    pallas_call x1, Pallas kernels, local_gram(): pl.pallas_call(gram_kernel, grid=(width // CHUNK,), out_shape=(jax.ShapeD...  8.95 us

profile of v1, /device:TPU:1, one launch (start us, length us, event | category | flops | bytes accessed | tf_op | source)
XLA Modules:
  0.0 144.4 jit_solution(9877582130809206166)
XLA Ops:
  0.6 61.2 %exchange.1.arrived = bf16[128,4,4096]{2,1,0:T(4,128)(2,1)} custom-call(s32[1024]{0:T(1024)} %order.1, bf16[1024,4,512]{2,1,0:T(4,128)(2,1)} %bitcast.3), custom_call_target="tpu_custom_call" | custom-call | tf_op jit(solution)/shard_map/exchange/pallas_call | solution.py:216
  61.8 9.0 %local_gram.1 = (bf16[512,4096]{1,0:T(8,128)(2,1)}, f32[512,512]{1,0:T(8,128)}) custom-call(bf16[128,4,4096]{2,1,0:T(4,128)(2,1)} %exchange.1.arrived), custom_call_target="tpu_custom_call" | custom-call | tf_op jit(solution)/shard_map/local_gram/pallas_call | solution.py:255
  70.8 31.5 %sum_over_devices.1.gram = f32[512,512]{1,0:T(8,128)} custom-call(f32[512,512]{1,0:T(8,128)} %get-tuple-element.4.gram), custom_call_target="tpu_custom_call" | custom-call | tf_op jit(solution)/shard_map/sum_over_devices/pallas_call | solution.py:352
  102.3 41.9 %factor_and_basis.1 = (f32[512,512]{1,0:T(8,128)}, f32[512,4096]{1,0:T(8,128)}) custom-call(f32[512,512]{1,0:T(8,128)} %sum_over_devices.1.gram, bf16[512,4096]{1,0:T(8,128)(2,1)} %get-tuple-element.5.owned_hbm), custom_call_target="tpu_custom_call" | custom-call | tf_op jit(solution)/shard_map/factor_and_basis/pallas_call | solution.py:118

commit v2 on v1

v2 whole, which is shorter than its diff:
```python
import math, functools
import jax, jax.numpy as jnp
from jax import lax
from jax.experimental import pallas as pl
from jax.experimental.pallas import tpu as pltpu
from jax.sharding import PartitionSpec as P

TILE = 128
GROUP = 8
CHUNK = 1024
HALVES = 2
VMEM_BYTES = 56 * 2**20
MESH = pl.DeviceIdType.MESH
EXACT = lax.Precision.HIGHEST


def factor_tile(work):
    lanes = lax.broadcasted_iota(jnp.int32, (8, TILE), 1)
    subs = lax.broadcasted_iota(jnp.int32, (8, TILE), 0)
    nslab = TILE // 8
    left = [work[8 * s : 8 * s + 8, :] for s in range(nslab)]
    right = [(lanes == subs + 8 * s).astype(jnp.float32) for s in range(nslab)]
    upper_rows, inverse_rows = [], []
    for start in range(0, TILE, GROUP):
        slab, base = start // 8, start % 8
        rows = [jnp.broadcast_to(left[slab][base + k : base + k + 1, :], (8, TILE)) for k in range(GROUP)]
        sides = [jnp.broadcast_to(right[slab][base + k : base + k + 1, :], (8, TILE)) for k in range(GROUP)]
        columns = [
            [jnp.broadcast_to(left[s][:, start + k : start + k + 1], (8, TILE)) for k in range(GROUP)]
            for s in range(slab, nslab)
        ]
        corner = [
            [jnp.broadcast_to(rows[k][:, start + l : start + l + 1], (8, TILE)) if l >= k else None for l in range(GROUP)]
            for k in range(GROUP)
        ]
        for k in range(GROUP):
            root = lax.rsqrt(corner[k][k])
            rows[k] = rows[k] * root
            sides[k] = sides[k] * root
            for column in columns:
                column[k] = column[k] * root
            scaled = [corner[k][l] * root if l > k else None for l in range(GROUP)]
            for l in range(k + 1, GROUP):
                for m in range(l, GROUP):
                    corner[l][m] = corner[l][m] - scaled[l] * scaled[m]
                rows[l] = rows[l] - scaled[l] * rows[k]
                sides[l] = sides[l] - scaled[l] * sides[k]
                for column in columns:
                    column[l] = column[l] - scaled[l] * column[k]
            upper_rows.append(rows[k][:1, :])
            inverse_rows.append(sides[k][:1, :])
        first = slab + (1 if base + GROUP == 8 else 0)
        for s in range(first, nslab):
            column = columns[s - slab]
            new_left, new_right = left[s], right[s]
            for k in range(GROUP):
                new_left = new_left - column[k] * rows[k]
                new_right = new_right - column[k] * sides[k]
            left[s], right[s] = new_left, new_right
    upper = jnp.concatenate(upper_rows, axis=0)
    inverse = jnp.concatenate(inverse_rows, axis=0)
    return upper, inverse


def mul(a, b):
    return lax.dot_general(a, b, (((1,), (0,)), ((), ())), precision=EXACT, preferred_element_type=jnp.float32)


def mul_t(a, b):
    return lax.dot_general(a, b, (((0,), (0,)), ((), ())), precision=EXACT, preferred_element_type=jnp.float32)


def factor_kernel(gram, owned_hbm, factor, basis_hbm, work, side, narrow, owned, basis, owned_sem, basis_sem, *, root):
    size, width = owned.shape
    fetch = pltpu.make_async_copy(owned_hbm, owned, owned_sem)
    fetch.start()
    work[...] = gram[...]
    panels = size // TILE
    stores = []
    for p in range(panels):
        lo, hi = p * TILE, (p + 1) * TILE
        upper, inverse = factor_tile(work[lo:hi, lo:hi])
        rows = lax.broadcasted_iota(jnp.int32, (TILE, TILE), 0)
        lanes = lax.broadcasted_iota(jnp.int32, (TILE, TILE), 1)
        factor[lo:hi, lo:hi] = jnp.where(lanes >= rows, upper, 0.0) / root
        if p:
            factor[lo:hi, :lo] = jnp.zeros((TILE, lo), jnp.float32)
            inverse = jnp.concatenate([mul(inverse, side[lo:hi, :lo]), inverse], axis=1)
        if hi < size:
            cross = mul(inverse[:, lo:hi], work[lo:hi, hi:])
            factor[lo:hi, hi:] = cross / root
            work[hi:, hi:] = work[hi:, hi:] - mul_t(cross, cross)
            update = -mul_t(cross, inverse)
            if p:
                side[hi:, :lo] = side[hi:, :lo] + update[:, :lo]
            side[hi:, lo:hi] = update[:, lo:hi]
        narrow[lo:hi, :hi] = (inverse * root).astype(jnp.bfloat16)
        if hi < size:
            narrow[lo:hi, hi:] = jnp.zeros((TILE, size - hi), jnp.bfloat16)
        if p == 1:
            fetch.wait()
        if p % 2:
            first, parts = lo - TILE, 1 if hi < size else 4
            for c in range(parts):
                span = width // parts

                def columns(i, carry, first=first, hi=hi, start=c * span):
                    at = pl.ds(pl.multiple_of(start + i * CHUNK, CHUNK), CHUNK)
                    basis[first:hi, at] = jnp.dot(
                        narrow[first:hi, :hi], owned[:hi, at], preferred_element_type=jnp.float32
                    )
                    return carry

                lax.fori_loop(0, span // CHUNK, columns, 0)
                at = slice(c * span, (c + 1) * span)
                store = pltpu.make_async_copy(
                    basis.at[first:hi, at], basis_hbm.at[first:hi, at], basis_sem.at[len(stores)]
                )
                store.start()
                stores.append(store)
    for store in stores:
        store.wait()


def factor_and_basis(gram, owned, total_rows):
    size, width = owned.shape
    return pl.pallas_call(
        functools.partial(factor_kernel, root=math.sqrt(total_rows)),
        out_shape=(
            jax.ShapeDtypeStruct((size, size), jnp.float32),
            jax.ShapeDtypeStruct((size, width), jnp.float32),
        ),
        in_specs=[pl.BlockSpec(memory_space=pltpu.VMEM), pl.BlockSpec(memory_space=pl.ANY)],
        out_specs=(pl.BlockSpec(memory_space=pltpu.VMEM), pl.BlockSpec(memory_space=pl.ANY)),
        scratch_shapes=[
            pltpu.VMEM((size, size), jnp.float32),
            pltpu.VMEM((size, size), jnp.float32),
            pltpu.VMEM((size, size), jnp.bfloat16),
            pltpu.VMEM((size, width), jnp.bfloat16),
            pltpu.VMEM((size, width), jnp.float32),
            pltpu.SemaphoreType.DMA,
            pltpu.SemaphoreType.DMA((8,)),
        ],
        compiler_params=pltpu.CompilerParams(vmem_limit_bytes=VMEM_BYTES),
        name="factor_and_basis",
    )(gram, owned)


def position():
    row, col = lax.axis_index("row"), lax.axis_index("col")
    x, y = lax.div(row, 4), lax.div(col, 2)
    return row, col, x, row - 4 * x, y, col - 2 * y


def wrap(place):
    return jnp.where(place >= 4, place - 4, place)


def each_partner(place, both, visit):
    row, col, x, z, y, core = place
    ring = [y] + [wrap(y + d) for d in range(1, 4)]
    cores = [core, 1 - core] if both else [core]

    def turn(step, carry):
        outer = lax.div(step, 4)
        from_x, from_z = wrap(x + outer), wrap(z + step - 4 * outer)
        for d in range(4):
            there_row = wrap(from_x + d) * 4 + wrap(from_z + (4 - d) % 4)
            for c, there_core in enumerate(cores):
                there = (there_row, ring[d] * 2 + there_core)
                if d or c:
                    visit(there)
                else:
                    pl.when(step > 0)(functools.partial(visit, there))
        return carry

    lax.fori_loop(0, 16, turn, 0)


def exchange_kernel(
    order, snapshots_hbm, owned_hbm, total,
    snapshots, staged, arrived, owned, gram, half, parts, part,
    fetch_sem, own_sem, store_sem, block_send, block_recv,
    pair_send, pair_recv, send_sem, recv_sem, back_send, back_recv, last_send, last_recv,
):
    place = position()
    row, col, x, z, y, core = place
    pieces, count, depth, span = staged.shape
    me = row * 8 + col
    block = snapshots.shape[2]
    each = span // block
    size = gram.shape[0]
    middle = size // 2
    chips = parts.shape[0]
    sibling = (row, 2 * y + 1 - core)
    chip = row * 4 + y

    fetch = pltpu.make_async_copy(snapshots_hbm, snapshots, fetch_sem)
    fetch.start()
    barrier = pltpu.get_barrier_semaphore()

    def greet(there):
        pl.semaphore_signal(barrier, inc=1, device_id=there, device_id_type=MESH)

    each_partner(place, True, greet)
    fetch.wait()
    own = []
    for piece in range(pieces):

        def gather(there, carry, piece=piece):
            for k in range(each):
                staged[piece, there, :, k * block : (k + 1) * block] = snapshots[
                    order[(there * pieces + piece) * each + k]
                ]
            return carry

        lax.fori_loop(0, count, gather, 0)
        if piece == 0:
            pl.semaphore_wait(barrier, count - 1)

        def send_block(there, piece=piece):
            pltpu.make_async_remote_copy(
                src_ref=staged.at[piece, there[0] * 8 + there[1]],
                dst_ref=arrived.at[piece, me],
                send_sem=block_send.at[piece],
                recv_sem=block_recv.at[piece],
                device_id=there,
                device_id_type=MESH,
            ).start()

        each_partner(place, True, send_block)
        copy = pltpu.make_async_copy(staged.at[piece, me], arrived.at[piece, me], own_sem.at[piece])
        copy.start()
        own.append(copy)

    stores = []
    for piece in range(pieces):
        own[piece].wait()
        blocks = staged.at[piece, pl.ds(0, count - 1)]
        pltpu.make_async_copy(blocks, blocks, block_recv.at[piece]).wait()
        for c in range(span // CHUNK):
            got = arrived[piece, :, :, c * CHUNK : (c + 1) * CHUNK].reshape(size, CHUNK)
            owned[:, piece * span + c * CHUNK : piece * span + (c + 1) * CHUNK] = got
            product = lax.dot_general(
                got, got, (((1,), (1,)), ((), ())), preferred_element_type=jnp.float32
            )
            gram[...] = product if piece == 0 and c == 0 else gram[...] + product
        at = slice(piece * span, (piece + 1) * span)
        store = pltpu.make_async_copy(owned.at[:, at], owned_hbm.at[:, at], store_sem.at[piece])
        store.start()
        stores.append(store)

    mine = pl.multiple_of(core * middle, middle)
    theirs = pl.multiple_of((1 - core) * middle, middle)
    pair = pltpu.make_async_remote_copy(
        src_ref=gram.at[pl.ds(theirs, middle)],
        dst_ref=half,
        send_sem=pair_send,
        recv_sem=pair_recv,
        device_id=sibling,
        device_id_type=MESH,
    )
    pair.start()
    pair.wait()
    half[...] = half[...] + gram[pl.ds(mine, middle), :]

    def send(there):
        top, left = pl.multiple_of(there[0] * 16, 16), pl.multiple_of((there[1] - core) * 64, 128)
        pltpu.make_async_remote_copy(
            src_ref=half.at[pl.ds(top, 16), pl.ds(left, 128)],
            dst_ref=parts.at[chip],
            send_sem=send_sem,
            recv_sem=recv_sem,
            device_id=there,
            device_id_type=MESH,
        ).start()

    each_partner(place, False, send)
    top, left = pl.multiple_of(row * 16, 16), pl.multiple_of(y * 128, 128)
    parts[chip] = half[pl.ds(top, 16), pl.ds(left, 128)]
    others = parts.at[pl.ds(0, chips - 1)]
    pltpu.make_async_copy(others, others, send_sem).wait()
    pltpu.make_async_copy(others, others, recv_sem).wait()
    sum_parts = parts[0]
    for k in range(1, chips):
        sum_parts = sum_parts + parts[k]
    part[...] = sum_parts
    total[pl.ds(mine + top, 16), pl.ds(left, 128)] = sum_parts

    def back(there):
        pltpu.make_async_remote_copy(
            src_ref=part,
            dst_ref=total.at[pl.ds(mine + top, 16), pl.ds(left, 128)],
            send_sem=back_send,
            recv_sem=back_recv,
            device_id=there,
            device_id_type=MESH,
        ).start()

    each_partner(place, False, back)
    pltpu.make_async_copy(others, others, back_send).wait()
    pltpu.make_async_copy(others, others, back_recv).wait()
    last = pltpu.make_async_remote_copy(
        src_ref=total.at[pl.ds(mine, middle)],
        dst_ref=total.at[pl.ds(mine, middle)],
        send_sem=last_send,
        recv_sem=last_recv,
        device_id=sibling,
        device_id_type=MESH,
    )
    last.start()
    last.wait()
    for piece in range(pieces):
        blocks = staged.at[piece, pl.ds(0, count - 1)]
        pltpu.make_async_copy(blocks, blocks, block_send.at[piece]).wait()
        stores[piece].wait()


def exchange(snapshots, block_order, devices):
    nblocks, local_count, block_rows = snapshots.shape
    size, width = devices * local_count, nblocks * block_rows // devices
    chips = devices // 2
    landing = pltpu.VMEM((HALVES, devices, local_count, width // HALVES), snapshots.dtype)
    return pl.pallas_call(
        exchange_kernel,
        out_shape=(
            jax.ShapeDtypeStruct((size, width), snapshots.dtype),
            jax.ShapeDtypeStruct((size, size), jnp.float32),
        ),
        in_specs=[pl.BlockSpec(memory_space=pltpu.SMEM), pl.BlockSpec(memory_space=pl.ANY)],
        out_specs=(pl.BlockSpec(memory_space=pl.ANY), pl.BlockSpec(memory_space=pltpu.VMEM)),
        scratch_shapes=[
            pltpu.VMEM(snapshots.shape, snapshots.dtype),
            landing,
            landing,
            pltpu.VMEM((size, width), snapshots.dtype),
            pltpu.VMEM((size, size), jnp.float32),
            pltpu.VMEM((size // 2, size), jnp.float32),
            pltpu.VMEM((chips, 16, 128), jnp.float32),
            pltpu.VMEM((16, 128), jnp.float32),
            pltpu.SemaphoreType.DMA,
            pltpu.SemaphoreType.DMA((HALVES,)),
            pltpu.SemaphoreType.DMA((HALVES,)),
            pltpu.SemaphoreType.DMA((HALVES,)),
            pltpu.SemaphoreType.DMA((HALVES,)),
        ]
        + [pltpu.SemaphoreType.DMA] * 8,
        compiler_params=pltpu.CompilerParams(
            collective_id=0, has_side_effects=True, vmem_limit_bytes=VMEM_BYTES
        ),
        name="exchange",
    )(block_order, snapshots)


def per_device(snapshots, block_order, devices):
    local_count, total_rows = snapshots.shape
    nblocks = block_order.shape[0]
    blocks = snapshots.reshape(local_count, nblocks, total_rows // nblocks).transpose(1, 0, 2)
    owned, summed = exchange(blocks, block_order, devices)
    return factor_and_basis(summed, owned, total_rows)


def solution(mesh):
    placed = (P(("row", "col"), None), P())
    return jax.shard_map(
        functools.partial(per_device, devices=mesh.size),
        mesh=mesh,
        in_specs=placed,
        out_specs=(P(), P(None, ("row", "col"))),
        check_vma=False,
    )
```

time: 145 us -> 117 us (0.81)
  Pallas kernels: 144 us -> 116 us
    pallas_call x3 -> x1, Pallas kernels: 102 us -> 86.5 us  [exchange(): pl.pallas_call(exchange_kernel, out_shape=(jax.ShapeDtypeStruct((size, wi...]
    pallas_call x1, Pallas kernels: 41.9 us -> 29.8 us  [factor_and_basis(): pl.pallas_call(functools.partial(factor_kernel, root=math.sqrt(total_rows...]
where the time goes in v2:
time: 117 us
  Pallas kernels  116 us (99%)
    pallas_call x1, Pallas kernels, exchange(): pl.pallas_call(exchange_kernel, out_shape=(jax.ShapeDtypeStruct((size, wi...  86.5 us
    pallas_call x1, Pallas kernels, factor_and_basis(): pl.pallas_call(functools.partial(factor_kernel, root=math.sqrt(total_rows...  29.8 us

profile of v2, /device:TPU:1, one launch (start us, length us, event | category | flops | bytes accessed | tf_op | source)
XLA Modules:
  0.0 117.1 jit_solution(12144125946513971961)
XLA Ops:
  0.6 86.5 %exchange.1 = (bf16[512,4096]{1,0:T(8,128)(2,1)}, f32[512,512]{1,0:T(8,128)}) custom-call(s32[1024]{0:T(1024)} %order.1, bf16[1024,4,512]{2,1,0:T(4,128)(2,1)} %bitcast.3), custom_call_target="tpu_custom_call" | custom-call | tf_op jit(solution)/shard_map/exchange/pallas_call | solution.py:324
  87.1 29.8 %factor_and_basis.1 = (f32[512,512]{1,0:T(8,128)}, f32[512,4096]{1,0:T(8,128)}) custom-call(f32[512,512]{1,0:T(8,128)} %get-tuple-element.4.gram, bf16[512,4096]{1,0:T(8,128)(2,1)} %get-tuple-element.5.owned_hbm), custom_call_target="tpu_custom_call" | custom-call | tf_op jit(solution)/shard_map/factor_and_basis/pallas_call | solution.py:127

commit v3 on v2

--- a/solution.py
+++ b/solution.py
@@ -177,9 +177,13 @@
     lax.fori_loop(0, 16, turn, 0)
 
 
+def upper_tiles(size):
+    return [(top, left) for top in range(0, size, TILE) for left in range(top, size, TILE)]
+
+
 def exchange_kernel(
     order, snapshots_hbm, owned_hbm, total,
-    snapshots, staged, arrived, owned, gram, half, parts, part,
+    snapshots, staged, arrived, owned, gram, packed, from_pair, half, parts, whole,
     fetch_sem, own_sem, store_sem, block_send, block_recv,
     pair_send, pair_recv, send_sem, recv_sem, back_send, back_recv, last_send, last_recv,
 ):
@@ -241,20 +245,23 @@
         for c in range(span // CHUNK):
             got = arrived[piece, :, :, c * CHUNK : (c + 1) * CHUNK].reshape(size, CHUNK)
             owned[:, piece * span + c * CHUNK : piece * span + (c + 1) * CHUNK] = got
-            product = lax.dot_general(
-                got, got, (((1,), (1,)), ((), ())), preferred_element_type=jnp.float32
-            )
-            gram[...] = product if piece == 0 and c == 0 else gram[...] + product
+            for top in (0, middle):
+                product = lax.dot_general(
+                    got[top : top + middle], got[top:], (((1,), (1,)), ((), ())), preferred_element_type=jnp.float32
+                )
+                at = slice(top, top + middle), slice(top, size)
+                gram[at] = product if piece == 0 and c == 0 else gram[at] + product
         at = slice(piece * span, (piece + 1) * span)
         store = pltpu.make_async_copy(owned.at[:, at], owned_hbm.at[:, at], store_sem.at[piece])
         store.start()
         stores.append(store)
 
-    mine = pl.multiple_of(core * middle, middle)
-    theirs = pl.multiple_of((1 - core) * middle, middle)
+    tiles = upper_tiles(size)
+    for t, (top, left) in enumerate(tiles):
+        packed[t // 5, t % 5] = gram[top : top + TILE, left : left + TILE].reshape(TILE // 2, 2, TILE)
     pair = pltpu.make_async_remote_copy(
-        src_ref=gram.at[pl.ds(theirs, middle)],
-        dst_ref=half,
+        src_ref=packed.at[1 - core],
+        dst_ref=from_pair,
         send_sem=pair_send,
         recv_sem=pair_recv,
         device_id=sibling,
@@ -262,12 +269,11 @@
     )
     pair.start()
     pair.wait()
-    half[...] = half[...] + gram[pl.ds(mine, middle), :]
+    half[...] = packed[core].reshape(half.shape) + from_pair[...].reshape(half.shape)
 
     def send(there):
-        top, left = pl.multiple_of(there[0] * 16, 16), pl.multiple_of((there[1] - core) * 64, 128)
         pltpu.make_async_remote_copy(
-            src_ref=half.at[pl.ds(top, 16), pl.ds(left, 128)],
+            src_ref=half.at[there[0] * 4 + lax.div(there[1], 2)],
             dst_ref=parts.at[chip],
             send_sem=send_sem,
             recv_sem=recv_sem,
@@ -276,21 +282,19 @@
         ).start()
 
     each_partner(place, False, send)
-    top, left = pl.multiple_of(row * 16, 16), pl.multiple_of(y * 128, 128)
-    parts[chip] = half[pl.ds(top, 16), pl.ds(left, 128)]
+    parts[chip] = half[chip]
     others = parts.at[pl.ds(0, chips - 1)]
     pltpu.make_async_copy(others, others, send_sem).wait()
     pltpu.make_async_copy(others, others, recv_sem).wait()
-    sum_parts = parts[0]
+    summed = parts[0]
     for k in range(1, chips):
-        sum_parts = sum_parts + parts[k]
-    part[...] = sum_parts
-    total[pl.ds(mine + top, 16), pl.ds(left, 128)] = sum_parts
+        summed = summed + parts[k]
+    whole[core, chip] = summed
 
     def back(there):
         pltpu.make_async_remote_copy(
-            src_ref=part,
-            dst_ref=total.at[pl.ds(mine + top, 16), pl.ds(left, 128)],
+            src_ref=whole.at[core, chip],
+            dst_ref=whole.at[core, chip],
             send_sem=back_send,
             recv_sem=back_recv,
             device_id=there,
@@ -301,15 +305,19 @@
     pltpu.make_async_copy(others, others, back_send).wait()
     pltpu.make_async_copy(others, others, back_recv).wait()
     last = pltpu.make_async_remote_copy(
-        src_ref=total.at[pl.ds(mine, middle)],
-        dst_ref=total.at[pl.ds(mine, middle)],
+        src_ref=whole.at[core],
+        dst_ref=whole.at[core],
         send_sem=last_send,
         recv_sem=last_recv,
         device_id=sibling,
         device_id_type=MESH,
     )
     last.start()
+    total[...] = jnp.zeros_like(total)
     last.wait()
+    for t, (top, left) in enumerate(tiles):
+        tile = whole[t // 5].reshape(5, TILE // 2, 2, TILE)[t % 5]
+        total[top : top + TILE, left : left + TILE] = tile.reshape(TILE, TILE)
     for piece in range(pieces):
         blocks = staged.at[piece, pl.ds(0, count - 1)]
         pltpu.make_async_copy(blocks, blocks, block_send.at[piece]).wait()
@@ -335,9 +343,11 @@
             landing,
             pltpu.VMEM((size, width), snapshots.dtype),
             pltpu.VMEM((size, size), jnp.float32),
-            pltpu.VMEM((size // 2, size), jnp.float32),
-            pltpu.VMEM((chips, 16, 128), jnp.float32),
-            pltpu.VMEM((16, 128), jnp.float32),
+            pltpu.VMEM((2, 5, TILE // 2, 2, TILE), jnp.float32),
+            pltpu.VMEM((5, TILE // 2, 2, TILE), jnp.float32),
+            pltpu.VMEM((chips, 5, 2, TILE), jnp.float32),
+            pltpu.VMEM((chips, 5, 2, TILE), jnp.float32),
+            pltpu.VMEM((2, chips, 5, 2, TILE), jnp.float32),
             pltpu.SemaphoreType.DMA,
             pltpu.SemaphoreType.DMA((HALVES,)),
             pltpu.SemaphoreType.DMA((HALVES,)),

time: 117 us -> 113 us (0.966)
  Pallas kernels: 116 us -> 112 us
    pallas_call x1, Pallas kernels: 86.5 us -> 82.2 us  [exchange(): pl.pallas_call(exchange_kernel, out_shape=(jax.ShapeDtypeStruct((size, wi...]
where the time goes in v3:
time: 113 us
  Pallas kernels  112 us (99%)
    pallas_call x1, Pallas kernels, exchange(): pl.pallas_call(exchange_kernel, out_shape=(jax.ShapeDtypeStruct((size, wi...  82.2 us
    pallas_call x1, Pallas kernels, factor_and_basis(): pl.pallas_call(functools.partial(factor_kernel, root=math.sqrt(total_rows...  29.8 us

profile of v3, /device:TPU:1, one launch (start us, length us, event | category | flops | bytes accessed | tf_op | source)
XLA Modules:
  0.0 112.8 jit_solution(5742458049794815104)
XLA Ops:
  0.6 82.2 %exchange.1 = (bf16[512,4096]{1,0:T(8,128)(2,1)}, f32[512,512]{1,0:T(8,128)}) custom-call(s32[1024]{0:T(1024)} %order.1, bf16[1024,4,512]{2,1,0:T(4,128)(2,1)} %bitcast.3), custom_call_target="tpu_custom_call" | custom-call | tf_op jit(solution)/shard_map/exchange/pallas_call | solution.py:332
  82.8 29.8 %factor_and_basis.1 = (f32[512,512]{1,0:T(8,128)}, f32[512,4096]{1,0:T(8,128)}) custom-call(f32[512,512]{1,0:T(8,128)} %get-tuple-element.4.gram, bf16[512,4096]{1,0:T(8,128)(2,1)} %get-tuple-element.5.owned_hbm), custom_call_target="tpu_custom_call" | custom-call | tf_op jit(solution)/shard_map/factor_and_basis/pallas_call | solution.py:127

commit v4 on v3

--- a/solution.py
+++ b/solution.py
@@ -76,7 +76,7 @@
     fetch.start()
     work[...] = gram[...]
     panels = size // TILE
-    stores = []
+    stores, waiting = [], []
     for p in range(panels):
         lo, hi = p * TILE, (p + 1) * TILE
         upper, inverse = factor_tile(work[lo:hi, lo:hi])
@@ -99,23 +99,24 @@
             narrow[lo:hi, hi:] = jnp.zeros((TILE, size - hi), jnp.bfloat16)
         if p == 1:
             fetch.wait()
-        if p % 2:
-            first, parts = lo - TILE, 1 if hi < size else 4
-            for c in range(parts):
-                span = width // parts
-
-                def columns(i, carry, first=first, hi=hi, start=c * span):
-                    at = pl.ds(pl.multiple_of(start + i * CHUNK, CHUNK), CHUNK)
-                    basis[first:hi, at] = jnp.dot(
-                        narrow[first:hi, :hi], owned[:hi, at], preferred_element_type=jnp.float32
-                    )
-                    return carry
-
-                lax.fori_loop(0, span // CHUNK, columns, 0)
-                at = slice(c * span, (c + 1) * span)
-                store = pltpu.make_async_copy(
-                    basis.at[first:hi, at], basis_hbm.at[first:hi, at], basis_sem.at[len(stores)]
-                )
+        for store in waiting:
+            store.start()
+        stores += waiting
+        waiting = []
+        if p == 0:
+            continue
+        first = 0 if p == 1 else lo
+        for c in range(width // CHUNK):
+            at = slice(c * CHUNK, (c + 1) * CHUNK)
+            basis[first:hi, at] = jnp.dot(
+                narrow[first:hi, :hi], owned[:hi, at], preferred_element_type=jnp.float32
+            )
+            store = pltpu.make_async_copy(
+                basis.at[first:hi, at], basis_hbm.at[first:hi, at], basis_sem.at[p - 1, c]
+            )
+            if hi < size:
+                waiting.append(store)
+            else:
                 store.start()
                 stores.append(store)
     for store in stores:
@@ -139,7 +140,7 @@
             pltpu.VMEM((size, width), jnp.bfloat16),
             pltpu.VMEM((size, width), jnp.float32),
             pltpu.SemaphoreType.DMA,
-            pltpu.SemaphoreType.DMA((8,)),
+            pltpu.SemaphoreType.DMA((size // TILE - 1, width // CHUNK)),
         ],
         compiler_params=pltpu.CompilerParams(vmem_limit_bytes=VMEM_BYTES),
         name="factor_and_basis",

time: 113 us -> 111 us (0.982)
  Pallas kernels: 112 us -> 110 us
    pallas_call x1, Pallas kernels: 29.8 us -> 27.5 us  [factor_and_basis(): pl.pallas_call(functools.partial(factor_kernel, root=math.sqrt(total_rows...]
where the time goes in v4:
time: 111 us
  Pallas kernels  110 us (99%)
    pallas_call x1, Pallas kernels, exchange(): pl.pallas_call(exchange_kernel, out_shape=(jax.ShapeDtypeStruct((size, wi...  82.2 us
    pallas_call x1, Pallas kernels, factor_and_basis(): pl.pallas_call(functools.partial(factor_kernel, root=math.sqrt(total_rows...  27.5 us

profile of v4, /device:TPU:1, one launch (start us, length us, event | category | flops | bytes accessed | tf_op | source)
XLA Modules:
  0.0 110.6 jit_solution(11669867065379223543)
XLA Ops:
  0.6 82.2 %exchange.1 = (bf16[512,4096]{1,0:T(8,128)(2,1)}, f32[512,512]{1,0:T(8,128)}) custom-call(s32[1024]{0:T(1024)} %order.1, bf16[1024,4,512]{2,1,0:T(4,128)(2,1)} %bitcast.3), custom_call_target="tpu_custom_call" | custom-call | tf_op jit(solution)/shard_map/exchange/pallas_call | solution.py:333
  82.8 27.5 %factor_and_basis.1 = (f32[512,512]{1,0:T(8,128)}, f32[512,4096]{1,0:T(8,128)}) custom-call(f32[512,512]{1,0:T(8,128)} %get-tuple-element.4.gram, bf16[512,4096]{1,0:T(8,128)(2,1)} %get-tuple-element.5.owned_hbm), custom_call_target="tpu_custom_call" | custom-call | tf_op jit(solution)/shard_map/factor_and_basis/pallas_call | solution.py:128
